TPU v7x, 32 devices: a whole 2x2x4 slice. The times are simulated.
32 devices in a mesh: row: 8 (over y, x, core), col: 4 (over z).
Axes of the slice: x: 2, y: 2, z: 4, core: 2. Of those that a mesh axis runs over, the one named last changes fastest.
Arguments:
- slab: float32 [4096, 10240], P('row', 'col'), may hold values from -6 to 6
- leaf_y: float32 [4096, 256], P('row', 'col'), may hold values from -0.25 to 0.25
- leaf_t: float32 [2048, 256], P('row', 'col'), may hold values from -0.2 to 2.3, as said below
- tree_y: float32 [3, 2048, 256], P(None, 'row'), may hold values from -0.25 to 0.25
- tree_t: float32 [3, 2048, 256], P(None, 'row'), may hold values from -0.2 to 2.3, as said below
Outputs:
- result: float32 [4096, 10240], P('row', 'col')
Inputs may be any that keep to these rules, and one draw needn't show every extreme that they name: `leaf_t`: each 256 x 256 block is upper triangular, with diagonal entries between 1.7 and 2.3 and off-diagonal entries of magnitude at most 0.2. `tree_t`: each 256 x 256 block is upper triangular, with diagonal entries between 1.7 and 2.3 and off-diagonal entries of magnitude at most 0.2; blocks of a section s that do not belong to a node's lower member are not used.
All inputs are finite; a program needn't handle non-finite values.
Results may differ from a plain program's by a relative error of at most 0.0002.
Values sent between devices are 32-bit elements; how exact they have to be, the bound alone decides.
A program may use at most 64 MiB of HBM per device.

v0:
```python
import jax
import jax.numpy as jnp
from jax import lax
from jax.sharding import PartitionSpec as P


def swapped(block, axis, bit):
    count = lax.axis_size(axis)
    route = []
    for low in range(count):
        high = low | 1 << bit
        if high != low and high < count:
            route += [(low, high), (high, low)]
    return lax.ppermute(block, axis, route)


def contract(left, right):
    return lax.dot_general(
        left,
        right,
        (((0,), (0,)), ((), ())),
        precision=lax.Precision.HIGHEST,
        preferred_element_type=jnp.float32,
    )


def expand(vectors, scaled):
    return jnp.dot(
        vectors, scaled, precision=lax.Precision.HIGHEST, preferred_element_type=jnp.float32
    )


def shards(slab, leaf_y, leaf_t, tree_y, tree_t):
    leaf_full, leaf_tri = (
        lax.all_gather(leaf_y, "col", axis=1, tiled=True),
        lax.all_gather(leaf_t, "col", axis=1, tiled=True),
    )
    width = leaf_tri.shape[0]
    coeffs = contract(leaf_full, slab)
    scaled = contract(leaf_tri, coeffs)
    updated = slab - expand(leaf_full, scaled)
    head_rows = updated[:width]
    tail_rows = updated[width:]
    position = lax.axis_index("row")
    for section in range(tree_y.shape[0]):
        stride = 2**section
        active = position % stride == 0
        is_lower = position % (2 * stride) == 0
        own_y = tree_y[section]
        own_t = tree_t[section]
        own_part = contract(own_y, head_rows)
        partner_part, partner_t = swapped((own_part, own_t), "row", section)
        node_coeffs = own_part + partner_part
        node_t = jnp.where(is_lower, own_t, partner_t)
        node_scaled = contract(node_t, node_coeffs)
        head_rows = jnp.where(active, head_rows - expand(own_y, node_scaled), head_rows)
    return jnp.concatenate([head_rows, tail_rows], axis=0)


def solution(mesh):
    in_specs = (
        P("row", "col"),
        P("row", "col"),
        P("row", "col"),
        P(None, "row", None),
        P(None, "row", None),
    )
    out_specs = P("row", "col")
    return jax.shard_map(shards, mesh=mesh, in_specs=in_specs, out_specs=out_specs, check_vma=False)
```

profile of v0, /device:TPU:0, one launch (start us, length us, event | category | flops | bytes accessed | tf_op | source)
XLA Modules:
  0.0 232.6 jit_solution(14218208823335364874)
XLA Ops:
  0.0 17.6 %all_gather.6 = f32[512,256]{0,1:T(8,128)S(1)} all-gather(f32[512,64]{0,1:T(8,128)} %param.6), channel_id=1, replica_groups=mesh['row'=8,'col'=4] {'col'}, dimensions={1}, use_global_device_ids=true | all-gather | bytes 655360 | tf_op jit(solution)/shard_map/all_gather | solution.py:35
  17.6 0.0 slice-start.3
  17.6 15.0 %all_gather.7 = f32[256,256]{0,1:T(8,128)S(1)} all-gather(f32[256,64]{0,1:T(8,128)} %param.7), channel_id=1, replica_groups=mesh['row'=8,'col'=4] {'col'}, dimensions={1}, use_global_device_ids=true | all-gather | bytes 327680 | tf_op jit(solution)/shard_map/all_gather | solution.py:36
  32.6 0.0 slice-start.4
  32.6 6.7 %fusion.30 = f32[256,2560]{1,0:T(8,128)S(1)} fusion(f32[512,256]{0,1:T(8,128)S(1)} %all_gather.6, f32[512,2560]{1,0:T(8,128)} %param.5), kind=kOutput, calls=%fused_computation.41 | convolution fusion | flops 4026531840 | bytes 8388608 | tf_op jit(solution)/shard_map/dot_general | solution.py:18
  39.3 4.5 %fusion.31 = f32[2560,256]{1,0:T(8,128)S(1)} fusion(f32[256,2560]{1,0:T(8,128)S(1)} %fusion.30, f32[256,256]{0,1:T(8,128)S(1)} %all_gather.7), kind=kOutput, calls=%fused_computation.42 | convolution fusion | flops 2013265920 | bytes 5505024 | tf_op jit(solution)/shard_map/dot_general | solution.py:18
  43.8 0.0 slice-done.3
  43.8 0.0 slice-done.4
  43.9 0.0 copy-start.4
  43.9 4.4 %bitcast_subtract_fusion = f32[512,2560]{1,0:T(8,128)S(1)} fusion(f32[512,2560]{1,0:T(8,128)S(1)} %bitcast.68, f32[2560,256]{1,0:T(8,128)S(1)} %fusion.31, f32[512,256]{0,1:T(8,128)S(1)} %all_gather.6), kind=kOutput, calls=%fused_computation.1 | convolution fusion | flops 4027842560 | bytes 13631488 | tf_op jit(solution)/shard_map/dot_general | solution.py:28
  48.3 0.0 copy-done.4
  48.3 0.0 copy-start
  48.3 0.0 copy-start.3
  48.3 6.0 %convolution_bitcast_fusion.5 = f32[256,2560]{0,1:T(8,128)} fusion(f32[512,2560]{1,0:T(8,128)S(1)} %bitcast_subtract_fusion, f32[3,256,256]{2,1,0:T(8,128)S(1)} %copy-done.4), kind=kOutput, calls=%fused_computation.12 | convolution fusion | flops 2013265920 | bytes 5505024 | tf_op jit(solution)/shard_map/dot_general | solution.py:18
  54.3 0.0 copy-done
  54.3 0.0 collective-permute-start.1
  54.3 0.0 copy-done.3
  54.3 0.0 slice-start
  54.3 0.9 slice_bitcast_fusion
  55.2 0.5 collective-permute-start
  55.6 0.0 slice-start.1
  55.6 3.9 %collective-permute-done = f32[256,256]{1,0:T(8,128)S(1)} collective-permute-done((f32[256,256]{1,0:T(8,128)S(1)}, f32[256,256]{1,0:T(8,128)S(1)}, u32[]{:S(2)}, u32[]{:S(2)}) %collective-permute-start) | collective-permute-done | bytes 262176 | tf_op jit(solution)/shard_map/ppermute | solution.py:14
  59.5 0.0 collective-permute-done.1
  59.6 6.9 %fusion.9 = f32[256,2560]{1,0:T(8,128)S(1)} fusion(f32[256,2560]{0,1:T(8,128)} %convolution_bitcast_fusion.5, f32[256,2560]{0,1:T(8,128)} %collective-permute-done.1, f32[256,256]{1,0:T(8,128)S(1)} %collective-permute-done, pred[]{:T(512)S(6)} %eq.20, f32[3,256,256]{2,1,0:T(8,128)S(1)} %copy-done.3), kind=kOutput, calls=%fused_computation.17 | convolution fusion | flops 2013986816 | bytes 8388609 | tf_op jit(solution)/shard_map/dot_general | solution.py:18
  66.5 0.0 slice-done
  66.5 0.0 slice-done.1
  66.5 2.7 %fusion.4 = f32[256,2560]{1,0:T(8,128)S(1)} fusion(f32[256,2560]{1,0:T(8,128)S(1)} %fusion.9, f32[512,2560]{1,0:T(8,128)S(1)} %bitcast.66, f32[3,256,256]{2,1,0:T(8,128)S(1)} %copy-done.4), kind=kOutput, calls=%fused_computation.11 | convolution fusion | flops 2013921280 | bytes 8126464 | tf_op jit(solution)/shard_map/dot_general | solution.py:28
  69.2 0.0 copy-start.1
  69.2 6.0 %convolution_bitcast_fusion.3 = f32[256,2560]{0,1:T(8,128)S(1)} fusion(f32[256,2560]{1,0:T(8,128)S(1)} %fusion.4, f32[3,256,256]{2,1,0:T(8,128)} %param.8), kind=kOutput, calls=%fused_computation.9 | convolution fusion | flops 2013265920 | bytes 5505024 | tf_op jit(solution)/shard_map/dot_general | solution.py:18
  75.3 0.0 copy-done.1
  75.3 1.6 collective-permute-start.3
  76.8 0.5 collective-permute-start.2
  77.4 0.0 copy-start.2
  77.4 0.0 copy-start.5
  77.4 62.6 %collective-permute-done.2 = f32[256,256]{1,0:T(8,128)} collective-permute-done((f32[256,256]{1,0:T(8,128)}, f32[256,256]{1,0:T(8,128)}, u32[]{:S(2)}, u32[]{:S(2)}) %collective-permute-start.2) | collective-permute-done | bytes 262176 | tf_op jit(solution)/shard_map/ppermute | solution.py:14
  140.0 0.0 collective-permute-done.3
  140.0 6.1 %fusion.7 = f32[256,2560]{1,0:T(8,128)S(1)} fusion(f32[256,2560]{0,1:T(8,128)S(1)} %convolution_bitcast_fusion.3, f32[256,2560]{0,1:T(8,128)} %collective-permute-done.3, f32[256,256]{1,0:T(8,128)} %collective-permute-done.2, pred[]{:T(512)S(6)} %eq.19, f32[3,256,256]{2,1,0:T(8,128)S(1)} %copy-done.3), kind=kOutput, calls=%fused_computation.15 | convolution fusion | flops 2013986816 | bytes 8388609 | tf_op jit(solution)/shard_map/dot_general | solution.py:18
  146.1 0.0 copy-done.2
  146.1 0.0 copy-done.5
  146.1 2.7 %fusion.3 = f32[256,2560]{1,0:T(8,128)S(1)} fusion(f32[256,2560]{1,0:T(8,128)S(1)} %copy-done.2, f32[256,2560]{1,0:T(8,128)S(1)} %fusion.7, pred[]{:T(512)S(6)} %eq.20, f32[3,256,256]{2,1,0:T(8,128)S(1)} %copy-done.5), kind=kOutput, calls=%fused_computation.8 | convolution fusion | flops 2014576640 | bytes 8126465 | tf_op jit(solution)/shard_map/dot_general | solution.py:28
  148.9 5.8 %convolution_bitcast_fusion.1 = f32[256,2560]{0,1:T(8,128)} fusion(f32[256,2560]{1,0:T(8,128)S(1)} %fusion.3, f32[3,256,256]{2,1,0:T(8,128)S(1)} %copy-done.5), kind=kOutput, calls=%fused_computation.5 | convolution fusion | flops 2013265920 | bytes 5505024 | tf_op jit(solution)/shard_map/dot_general | solution.py:18
  154.6 1.5 collective-permute-start.5
  156.1 0.5 collective-permute-start.4
  156.7 62.1 %collective-permute-done.4 = f32[256,256]{1,0:T(8,128)} collective-permute-done((f32[256,256]{1,0:T(8,128)}, f32[256,256]{1,0:T(8,128)}, u32[]{:S(2)}, u32[]{:S(2)}) %collective-permute-start.4) | collective-permute-done | bytes 262176 | tf_op jit(solution)/shard_map/ppermute | solution.py:14
  218.7 0.0 collective-permute-done.5
  218.7 7.1 %fusion.5 = f32[256,2560]{1,0:T(8,128)S(1)} fusion(f32[256,2560]{0,1:T(8,128)} %convolution_bitcast_fusion.1, f32[256,2560]{0,1:T(8,128)} %collective-permute-done.5, f32[256,256]{1,0:T(8,128)} %collective-permute-done.4, pred[]{:T(512)S(6)} %eq.21, f32[3,256,256]{2,1,0:T(8,128)S(1)} %copy-done.3), kind=kOutput, calls=%fused_computation.13 | convolution fusion | flops 2013986816 | bytes 8388609 | tf_op jit(solution)/shard_map/dot_general | solution.py:18
  225.8 0.0 slice-start.2
  225.9 3.9 %fusion.1 = f32[256,2560]{1,0:T(8,128)S(1)} fusion(f32[256,2560]{1,0:T(8,128)S(1)} %fusion.3, f32[256,2560]{1,0:T(8,128)S(1)} %fusion.5, pred[]{:T(512)S(6)} %eq.19, f32[3,256,256]{2,1,0:T(8,128)} %param.8), kind=kOutput, calls=%fused_computation.4 | convolution fusion | flops 2014576640 | bytes 8126465 | tf_op jit(solution)/shard_map/dot_general | solution.py:28
  229.7 0.0 slice-done.2
  229.8 2.7 %pad_maximum_fusion = f32[512,2560]{1,0:T(8,128)} fusion(f32[256,2560]{1,0:T(8,128)S(1)} %slice-done.2, f32[256,2560]{1,0:T(8,128)S(1)} %fusion.1), kind=kLoop, calls=%fused_computation | loop fusion | flops 1310720 | bytes 10485760 | tf_op jit(solution)/shard_map/concatenate | solution.py:57
  (2 shorter events, 0.0 us)
Async XLA Ops:
  17.6 26.3 %slice-start.3 = ((s8[5242880]{0:T(1024)(128)(4,1)}), s8[4194304]{0:T(1024)(128)(4,1)S(1)}, s32[]{:S(2)}) async-start(s8[5242880]{0:T(1024)(128)(4,1)} %bitcast.67), calls=%async_computation.3 | async-start | bytes 8388608
  32.6 11.2 %slice-start.4 = ((s8[5242880]{0:T(1024)(128)(4,1)}), s8[1048576]{0:T(1024)(128)(4,1)S(1)}, s32[]{:S(2)}) async-start(s8[5242880]{0:T(1024)(128)(4,1)} %bitcast.67), calls=%async_computation.4 | async-start | bytes 2097152
  43.9 4.4 %copy-start.4 = (f32[3,256,256]{2,1,0:T(8,128)S(1)}, f32[3,256,256]{2,1,0:T(8,128)}, u32[]{:S(2)}) copy-start(f32[3,256,256]{2,1,0:T(8,128)} %param.8) | copy-start | bytes 2359300
  48.3 6.0 %copy-start = (f32[512,2560]{1,0:T(8,128)}, f32[512,2560]{1,0:T(8,128)S(1)}, u32[]{:S(2)}) copy-start(f32[512,2560]{1,0:T(8,128)S(1)} %bitcast_subtract_fusion) | copy-start | bytes 15728644
  48.3 6.0 %copy-start.3 = (f32[3,256,256]{2,1,0:T(8,128)S(1)}, f32[3,256,256]{2,1,0:T(8,128)}, u32[]{:S(2)}) copy-start(f32[3,256,256]{2,1,0:T(8,128)} %param.9) | copy-start | bytes 2359300
  54.3 5.3 %collective-permute-start.1 = (f32[256,2560]{0,1:T(8,128)}, f32[256,2560]{0,1:T(8,128)}, u32[]{:S(2)}, u32[]{:S(2)}) collective-permute-start(f32[256,2560]{0,1:T(8,128)} %convolution_bitcast_fusion.5), channel_id=1, source_target_pairs={{0,4},{4,0},{8,12},{12,8},{16,20},{20,16},{24,28},{28,24},{1,5},{5... | collective-permute-start | bytes 7864328 | tf_op jit(solution)/shard_map/ppermute | solution.py:14
  54.3 12.2 %slice-start = ((s8[5242880]{0:T(1024)(128)(4,1)}), s8[1048576]{0:T(1024)(128)(4,1)S(1)}, s32[]{:S(2)}) async-start(s8[5242880]{0:T(1024)(128)(4,1)} %bitcast.65), calls=%async_computation | async-start | bytes 2097152
  55.2 4.4 %collective-permute-start = (f32[256,256]{1,0:T(8,128)S(1)}, f32[256,256]{1,0:T(8,128)S(1)}, u32[]{:S(2)}, u32[]{:S(2)}) collective-permute-start(f32[256,256]{1,0:T(8,128)S(1)} %get-tuple-element.6), channel_id=1, source_target_pairs={{0,4},{4,0},{8,12},{12,8},{16,20},{20,16},{24,28},{28,24},{1,5},{5... | collective-permute-start | bytes 786440 | tf_op jit(solution)/shard_map/ppermute | solution.py:14
  55.6 10.9 %slice-start.1 = ((s8[5242880]{0:T(1024)(128)(4,1)}), s8[4194304]{0:T(1024)(128)(4,1)S(1)}, s32[]{:S(2)}) async-start(s8[5242880]{0:T(1024)(128)(4,1)} %bitcast.65), calls=%async_computation.1 | async-start | bytes 8388608
  69.2 6.1 %copy-start.1 = (f32[256,2560]{1,0:T(8,128)}, f32[256,2560]{1,0:T(8,128)S(1)}, u32[]{:S(2)}) copy-start(f32[256,2560]{1,0:T(8,128)S(1)} %fusion.4) | copy-start | bytes 7864324
  75.3 64.7 %collective-permute-start.3 = (f32[256,2560]{0,1:T(8,128)S(1)}, f32[256,2560]{0,1:T(8,128)}, u32[]{:S(2)}, u32[]{:S(2)}) collective-permute-start(f32[256,2560]{0,1:T(8,128)S(1)} %convolution_bitcast_fusion.3), channel_id=1, source_target_pairs={{0,8},{8,0},{4,12},{12,4},{16,24},{24,16},{20,28},{28,20},{1,9},{9... | collective-permute-start | bytes 7864328 | tf_op jit(solution)/shard_map/ppermute | solution.py:14
  76.8 63.1 %collective-permute-start.2 = (f32[256,256]{1,0:T(8,128)}, f32[256,256]{1,0:T(8,128)}, u32[]{:S(2)}, u32[]{:S(2)}) collective-permute-start(f32[256,256]{1,0:T(8,128)} %get-tuple-element.7), channel_id=1, source_target_pairs={{0,8},{8,0},{4,12},{12,4},{16,24},{24,16},{20,28},{28,20},{1,9},{9... | collective-permute-start | bytes 786440 | tf_op jit(solution)/shard_map/ppermute | solution.py:14
  77.4 68.8 %copy-start.2 = (f32[256,2560]{1,0:T(8,128)S(1)}, f32[256,2560]{1,0:T(8,128)}, u32[]{:S(2)}) copy-start(f32[256,2560]{1,0:T(8,128)} %copy-done.1) | copy-start | bytes 7864324
  77.4 68.8 %copy-start.5 = (f32[3,256,256]{2,1,0:T(8,128)S(1)}, f32[3,256,256]{2,1,0:T(8,128)}, u32[]{:S(2)}) copy-start(f32[3,256,256]{2,1,0:T(8,128)} %param.8) | copy-start | bytes 2359300
  154.6 64.1 %collective-permute-start.5 = (f32[256,2560]{0,1:T(8,128)}, f32[256,2560]{0,1:T(8,128)}, u32[]{:S(2)}, u32[]{:S(2)}) collective-permute-start(f32[256,2560]{0,1:T(8,128)} %convolution_bitcast_fusion.1), channel_id=1, source_target_pairs={{0,16},{16,0},{4,20},{20,4},{8,24},{24,8},{12,28},{28,12},{1,17},{... | collective-permute-start | bytes 7864328 | tf_op jit(solution)/shard_map/ppermute | solution.py:14
  156.1 62.6 %collective-permute-start.4 = (f32[256,256]{1,0:T(8,128)}, f32[256,256]{1,0:T(8,128)}, u32[]{:S(2)}, u32[]{:S(2)}) collective-permute-start(f32[256,256]{1,0:T(8,128)} %get-tuple-element.5), channel_id=1, source_target_pairs={{0,16},{16,0},{4,20},{20,4},{8,24},{24,8},{12,28},{28,12},{1,17},{... | collective-permute-start | bytes 786440 | tf_op jit(solution)/shard_map/ppermute | solution.py:14
  225.8 3.9 %slice-start.2 = ((f32[512,2560]{1,0:T(8,128)}), f32[256,2560]{1,0:T(8,128)S(1)}, s32[]{:S(2)}) async-start(f32[512,2560]{1,0:T(8,128)} %copy-done), calls=%async_computation.2 | async-start | bytes 5242880 | tf_op jit(solution)/shard_map/slice | solution.py:43
where the time goes:
time: 235 us; the launch traced here: 233 us
  waiting for transfers between devices  129 us (55%)
  matrix products  62.8 us (27%)
  blocking collectives  32.6 us (14%)
  starting transfers between devices  4.61 us (2%)
  other arithmetic  2.7 us (1%)
    ppermute x6, waiting for transfers between devices, swapped(): return lax.ppermute(block, axis, route)  129 us
    dot_general x8, matrix products, contract(): lax.dot_general(left, right, (((0,), (0,)), ((), ())), precision=lax.Prec...  49.1 us
    all_gather x1, blocking collectives, shards(): lax.all_gather(leaf_y, 'col', axis=1, tiled=True)  17.6 us
    all_gather x1, blocking collectives, shards(): lax.all_gather(leaf_t, 'col', axis=1, tiled=True)  15 us
    dot_general x4, matrix products, expand(): jnp.dot(vectors, scaled, precision=lax.Precision.HIGHEST, preferred_eleme...  13.7 us
  transfers between devices with their start and end apart: 6, of which 3 were waited for; matrix products, arithmetic and copies ran while one was open for 0% of the time, Pallas kernels for 0%

commit v1 on v0

v1 whole, which is shorter than its diff:
```python
import functools

import jax
import jax.numpy as jnp
from jax import lax
from jax.experimental import pallas as pl
from jax.experimental.pallas import tpu as pltpu
from jax.sharding import PartitionSpec as P

MESH = pl.DeviceIdType.MESH


def halves(x):
    high = x.astype(jnp.bfloat16)
    return high, (x - high.astype(jnp.float32)).astype(jnp.bfloat16)


def dot3(left, right, dims=((1,), (0,))):
    def one(a, b):
        return lax.dot_general(a, b, (dims, ((), ())), preferred_element_type=jnp.float32)

    return one(left[0], right[0]) + (one(left[0], right[1]) + one(left[1], right[0]))


def kernel(
    sizes,
    slab_hbm, leaf_y, leaf_t, tree_y_hbm, tree_t_hbm,
    out_hbm,
    slab, head, part_out, part_in, tree_y, tree_t,
    gather_y, gather_t, y_t, v, node_y_t, node_v,
    slab_sem, out_sem, part_send, part_recv, y_sem,
    t_local, t_send, t_recv, gather_send, gather_recv,
):
    peers, sections, chunks, width, chunk_cols, shard = sizes
    row, col = lax.axis_index("row"), lax.axis_index("col")
    partner = [jnp.bitwise_xor(row, 1 << s) for s in range(sections)]
    active = [lax.rem(row, 1 << s) == 0 for s in range(sections)]
    lower = [lax.rem(row, 2 << s) == 0 for s in range(sections)]

    def columns(c):
        return pl.ds(pl.multiple_of(c * chunk_cols, chunk_cols), chunk_cols)

    def slab_copy(c):
        return pltpu.make_async_copy(slab_hbm.at[:, columns(c)], slab.at[c], slab_sem.at[c])

    def tail_copy(c):
        return pltpu.make_async_copy(
            slab.at[c, pl.ds(width, width)], out_hbm.at[pl.ds(width, width), columns(c)], out_sem.at[1, c]
        )

    def head_copy(c):
        return pltpu.make_async_copy(
            head.at[c], out_hbm.at[pl.ds(0, width), columns(c)], out_sem.at[0, c]
        )

    def part_copy(s, c):
        return pltpu.make_async_remote_copy(
            src_ref=part_out.at[s, c], dst_ref=part_in.at[s, c],
            send_sem=part_send.at[s, c], recv_sem=part_recv.at[s, c],
            device_id={"row": partner[s]}, device_id_type=MESH,
        )

    def factor_copy(s):
        return pltpu.make_async_remote_copy(
            src_ref=tree_t_hbm.at[s], dst_ref=tree_t.at[s],
            send_sem=t_send.at[s], recv_sem=t_recv.at[s],
            device_id={"row": partner[s]}, device_id_type=MESH,
        )

    def factor_local(s):
        return pltpu.make_async_copy(tree_t_hbm.at[s], tree_t.at[s], t_local.at[s])

    mine = pl.ds(pl.multiple_of(col * shard, shard), shard)

    def gather_copy(which, d):
        buffer = (gather_y, gather_t)[which]
        return pltpu.make_async_remote_copy(
            src_ref=buffer.at[mine], dst_ref=buffer.at[mine],
            send_sem=gather_send.at[which, d], recv_sem=gather_recv.at[which, d],
            device_id={"col": lax.rem(col + d, peers)}, device_id_type=MESH,
        )

    barrier = pltpu.get_barrier_semaphore()
    for d in range(1, peers):
        pl.semaphore_signal(
            barrier, inc=1, device_id={"col": lax.rem(col + d, peers)}, device_id_type=MESH
        )
    for s in range(sections):
        pl.semaphore_signal(barrier, inc=1, device_id={"row": partner[s]}, device_id_type=MESH)

    y_copy = pltpu.make_async_copy(tree_y_hbm, tree_y, y_sem)
    y_copy.start()
    for s in range(sections):
        pl.when(lower[s])(lambda s=s: factor_local(s).start())
    for c in range(chunks):
        slab_copy(c).start()
    gather_y[mine, :] = leaf_y[...].T
    gather_t[mine, :] = leaf_t[...].T

    pl.semaphore_wait(barrier, peers - 1 + sections)
    for which in range(2):
        for d in range(1, peers):
            gather_copy(which, d).start()
    for s in range(sections):
        pl.when(lower[s])(lambda s=s: factor_copy(s).start())

    y_copy.wait()
    for s in range(sections):
        pl.when(lower[s])(lambda s=s: factor_local(s).wait())
        pl.when(jnp.logical_and(active[s], jnp.logical_not(lower[s])))(
            lambda s=s: factor_copy(s).wait_recv()
        )

        @pl.when(active[s])
        def _(s=s):
            vectors = tree_y[s]
            node_y_t[s, 0], node_y_t[s, 1] = halves(vectors.T)
            product = dot3(halves(vectors), halves(tree_t[s]), ((1,), (1,)))
            node_v[s, 0], node_v[s, 1] = halves(product)

    for which in range(2):
        for d in range(1, peers):
            gather_copy(which, d).wait_recv()
    all_y_t = gather_y[...]
    y_t[0], y_t[1] = halves(all_y_t)
    product = dot3(halves(all_y_t.T), halves(gather_t[...]))
    v[0], v[1] = halves(product)

    def send_part(s, c, rows):
        part_out[s, c] = dot3((node_y_t[s, 0], node_y_t[s, 1]), halves(rows))
        part_copy(s, c).start()

    def leaf(c):
        slab_copy(c).wait()
        block = slab[c]
        coeffs = dot3((y_t[0], y_t[1]), halves(block))
        updated = block - dot3((v[0], v[1]), halves(coeffs))
        rows = updated[:width]
        head[c] = rows
        slab[c, width:, :] = updated[width:]
        tail_copy(c).start()
        send_part(0, c, rows)

    def node(s, c):
        part_copy(s, c).wait_recv()
        coeffs = part_out[s, c] + part_in[s, c]
        rows = head[c] - dot3((node_v[s, 0], node_v[s, 1]), halves(coeffs))
        head[c] = rows
        if s + 1 < sections:
            pl.when(active[s + 1])(lambda: send_part(s + 1, c, rows))
            pl.when(jnp.logical_not(active[s + 1]))(lambda: head_copy(c).start())
        else:
            head_copy(c).start()

    lag = [1 + 2 * s for s in range(sections)]

    def step(t, carry):
        pl.when(t < chunks)(lambda: leaf(t))
        for s in range(sections):
            c = t - lag[s]
            inside = jnp.logical_and(c >= 0, c < chunks)
            pl.when(jnp.logical_and(active[s], inside))(lambda s=s, c=c: node(s, c))
        return carry

    lax.fori_loop(0, chunks + lag[-1], step, 0)

    def finish(c, carry):
        tail_copy(c).wait()
        head_copy(c).wait()
        for s in range(sections):
            pl.when(active[s])(lambda s=s: part_copy(s, c).wait_send())
        return carry

    lax.fori_loop(0, chunks, finish, 0)
    for which in range(2):
        for d in range(1, peers):
            gather_copy(which, d).wait_send()
    for s in range(sections):
        pl.when(lower[s])(lambda s=s: factor_copy(s).wait_send())


def shards(slab, leaf_y, leaf_t, tree_y, tree_t):
    peers = lax.axis_size("col")
    rows, cols = slab.shape
    sections, width, _ = tree_y.shape
    shard = leaf_y.shape[1]
    chunk_cols = next(size for size in (256, 128) if cols % size == 0)
    chunks = cols // chunk_cols
    f32, bf16 = jnp.float32, jnp.bfloat16
    sizes = (peers, sections, chunks, width, chunk_cols, shard)
    any_space = pl.BlockSpec(memory_space=pl.ANY)
    vmem = pl.BlockSpec(memory_space=pltpu.VMEM)
    dma = pltpu.SemaphoreType.DMA
    flops = 4 * cols * width * (rows + sections * width) * 3
    return pl.pallas_call(
        functools.partial(kernel, sizes),
        out_shape=jax.ShapeDtypeStruct(slab.shape, f32),
        in_specs=[any_space, vmem, vmem, any_space, any_space],
        out_specs=any_space,
        scratch_shapes=[
            pltpu.VMEM((chunks, rows, chunk_cols), f32),
            pltpu.VMEM((chunks, width, chunk_cols), f32),
            pltpu.VMEM((sections, chunks, width, chunk_cols), f32),
            pltpu.VMEM((sections, chunks, width, chunk_cols), f32),
            pltpu.VMEM(tree_y.shape, f32),
            pltpu.VMEM(tree_t.shape, f32),
            pltpu.VMEM((width, rows), f32),
            pltpu.VMEM((width, width), f32),
            pltpu.VMEM((2, width, rows), bf16),
            pltpu.VMEM((2, rows, width), bf16),
            pltpu.VMEM((sections, 2, width, width), bf16),
            pltpu.VMEM((sections, 2, width, width), bf16),
            dma((chunks,)),
            dma((2, chunks)),
            dma((sections, chunks)),
            dma((sections, chunks)),
            dma,
            dma((sections,)),
            dma((sections,)),
            dma((sections,)),
            dma((2, peers)),
            dma((2, peers)),
        ],
        compiler_params=pltpu.CompilerParams(
            collective_id=0, has_side_effects=True, vmem_limit_bytes=52 * 2**20
        ),
        cost_estimate=pl.CostEstimate(
            flops=flops, bytes_accessed=8 * rows * cols, transcendentals=0
        ),
    )(slab, leaf_y, leaf_t, tree_y, tree_t)


def solution(mesh):
    in_specs = (
        P("row", "col"),
        P("row", "col"),
        P("row", "col"),
        P(None, "row", None),
        P(None, "row", None),
    )
    out_specs = P("row", "col")
    return jax.shard_map(shards, mesh=mesh, in_specs=in_specs, out_specs=out_specs, check_vma=False)
```

time: 235 us -> 74.9 us (0.32)
  waiting for transfers between devices: 129 us -> 0 us
  Pallas kernels: 0 us -> 65.1 us
  matrix products: 62.8 us -> 0 us
  blocking collectives: 32.6 us -> 0 us
  local copies, waits for them, and re-layouts: 0.92 us -> 9.41 us
  starting transfers between devices: 4.61 us -> 0 us
  other arithmetic: 2.7 us -> 0 us
    ppermute x6 -> x0, waiting for transfers between devices: 129 us -> none  [swapped(): return lax.ppermute(block, axis, route)]
    pallas_call x0 -> x1, Pallas kernels: none -> 65.1 us  [shards(): pl.pallas_call(functools.partial(kernel, sizes), out_shape=jax.ShapeDtype...]
    dot_general x12 -> x0, matrix products: 62.8 us -> none  [the longest x8 49.1 us: contract(): lax.dot_general(left, right, (((0,), (0,)), ((), ())), precision=lax.Prec...]
    all_gather x2 -> x0, blocking collectives: 32.6 us -> none  [the longest x1 17.6 us: shards(): lax.all_gather(leaf_y, 'col', axis=1, tiled=True)]
    unnamed x20 -> x7, local copies, waits for them, and re-layouts: 0.05 us -> 9.41 us
    ppermute x6 -> x0, starting transfers between devices: 4.61 us -> none  [swapped(): return lax.ppermute(block, axis, route)]
    concatenate x1 -> x0, other arithmetic: 2.7 us -> none  [shards(): return jnp.concatenate([head_rows, tail_rows], axis=0)]
  transfers between devices with their start and end apart: 6 -> 0, of which waited for: 3 -> 0; matrix products, arithmetic and copies ran while one was open for 0% -> 0% of each run, Pallas kernels for 0% -> 0%
where the time goes in v1:
time: 74.9 us; the launch traced here: 74.6 us
  Pallas kernels  65.1 us (87%)
  local copies, waits for them, and re-layouts  9.41 us (13%)
    pallas_call x1, Pallas kernels, shards(): pl.pallas_call(functools.partial(kernel, sizes), out_shape=jax.ShapeDtype...  65.1 us
    unnamed x7, local copies, waits for them, and re-layouts  9.41 us

profile of v1, /device:TPU:0, one launch (start us, length us, event | category | flops | bytes accessed | tf_op | source)
XLA Modules:
  0.0 74.6 jit_solution(12215486108158967369)
XLA Ops:
  0.0 0.9 %copy.7.leaf_t = f32[256,64]{1,0:T(8,128)S(1)} copy(f32[256,64]{0,1:T(8,128)} %param.7) | data formatting | bytes 131072 | tf_op args[2]
  0.9 1.0 %copy.6.leaf_y = f32[512,64]{1,0:T(8,128)S(1)} copy(f32[512,64]{0,1:T(8,128)} %param.6) | data formatting | bytes 262144 | tf_op args[1]
  2.0 0.0 copy-start
  2.0 1.1 %copy-done = f32[3,256,256]{2,1,0:T(8,128)S(1)} copy-done((f32[3,256,256]{2,1,0:T(8,128)S(1)}, f32[3,256,256]{2,1,0:T(8,128)}, u32[]{:S(2)}) %copy-start) | copy-done | bytes 786456
  3.1 0.0 copy-start.1
  3.1 1.1 %copy-done.1 = f32[3,256,256]{2,1,0:T(8,128)S(1)} copy-done((f32[3,256,256]{2,1,0:T(8,128)S(1)}, f32[3,256,256]{2,1,0:T(8,128)}, u32[]{:S(2)}) %copy-start.1) | copy-done | bytes 786456
  4.2 65.1 %shard_map.55 = f32[512,2560]{1,0:T(8,128)} custom-call(f32[512,2560]{1,0:T(8,128)} %slab_hbm.1, f32[512,64]{1,0:T(8,128)S(1)} %copy.6.leaf_y, f32[256,64]{1,0:T(8,128)S(1)} %copy.7.leaf_t, f32[3,256,256]{2,1,0:T(8,128)S(1)} %copy-done, f32[3,256,256]{2,1,0:T(8,128)S(1)} %copy-done.1), custom_call_target="tpu_custom_call" | custom-call | flops 10066329600 | bytes 10485760 | tf_op jit(solution)/shard_map/pallas_call | solution.py:195
  69.4 5.2 %copy.9 = f32[512,2560]{1,0:T(8,128)} copy(f32[512,2560]{1,0:T(8,128)} %shard_map.55) | data formatting | bytes 10485760
Async XLA Ops:
  2.0 1.1 %copy-start = (f32[3,256,256]{2,1,0:T(8,128)S(1)}, f32[3,256,256]{2,1,0:T(8,128)}, u32[]{:S(2)}) copy-start(f32[3,256,256]{2,1,0:T(8,128)} %tree_y_hbm.1) | copy-start | bytes 2359300
  3.1 1.1 %copy-start.1 = (f32[3,256,256]{2,1,0:T(8,128)S(1)}, f32[3,256,256]{2,1,0:T(8,128)}, u32[]{:S(2)}) copy-start(f32[3,256,256]{2,1,0:T(8,128)} %tree_t_hbm.1) | copy-start | bytes 2359300

commit v2 on v1

--- a/solution.py
+++ b/solution.py
@@ -27,7 +27,7 @@
     slab_hbm, leaf_y, leaf_t, tree_y_hbm, tree_t_hbm,
     out_hbm,
     slab, head, part_out, part_in, tree_y, tree_t,
-    gather_y, gather_t, y_t, v, node_y_t, node_v,
+    gather_y, gather_t, y_t, v, v_sum, node_y_t, node_v,
     slab_sem, out_sem, part_send, part_recv, y_sem,
     t_local, t_send, t_recv, gather_send, gather_recv,
 ):
@@ -70,15 +70,33 @@
     def factor_local(s):
         return pltpu.make_async_copy(tree_t_hbm.at[s], tree_t.at[s], t_local.at[s])
 
-    mine = pl.ds(pl.multiple_of(col * shard, shard), shard)
-
-    def gather_copy(which, d):
-        buffer = (gather_y, gather_t)[which]
-        return pltpu.make_async_remote_copy(
-            src_ref=buffer.at[mine], dst_ref=buffer.at[mine],
-            send_sem=gather_send.at[which, d], recv_sem=gather_recv.at[which, d],
+    short = peers % 2 == 0 and width % 256 == 0
+
+    def of(owner):
+        return pl.ds(pl.multiple_of(owner * shard, shard), shard)
+
+    def y_shard(d):
+        return pltpu.make_async_remote_copy(
+            src_ref=gather_y.at[of(col)], dst_ref=gather_y.at[of(col)],
+            send_sem=gather_send.at[0, d], recv_sem=gather_recv.at[0, d],
             device_id={"col": lax.rem(col + d, peers)}, device_id_type=MESH,
         )
+
+    def t_shard(d, kept):
+        block = gather_t.at[of(col), pl.ds(0, kept)]
+        return pltpu.make_async_remote_copy(
+            src_ref=block, dst_ref=block,
+            send_sem=gather_send.at[1, d], recv_sem=gather_recv.at[1, d],
+            device_id={"col": lax.rem(col + d, peers)}, device_id_type=MESH,
+        )
+
+    def by_shard(owner, act):
+        if short:
+            early = 2 * owner < peers
+            pl.when(early)(lambda: act(width // 2))
+            pl.when(jnp.logical_not(early))(lambda: act(width))
+        else:
+            act(width)
 
     barrier = pltpu.get_barrier_semaphore()
     for d in range(1, peers):
@@ -94,13 +112,18 @@
         pl.when(lower[s])(lambda s=s: factor_local(s).start())
     for c in range(chunks):
         slab_copy(c).start()
-    gather_y[mine, :] = leaf_y[...].T
-    gather_t[mine, :] = leaf_t[...].T
+    if short:
+        gather_t[pl.ds(0, width // 2), pl.ds(width // 2, width // 2)] = jnp.zeros(
+            (width // 2, width // 2), jnp.float32
+        )
+    gather_y[of(col), :] = leaf_y[...]
+    gather_t[of(col), :] = leaf_t[...]
 
     pl.semaphore_wait(barrier, peers - 1 + sections)
-    for which in range(2):
-        for d in range(1, peers):
-            gather_copy(which, d).start()
+    for d in range(1, peers):
+        y_shard(d).start()
+    for d in range(1, peers):
+        by_shard(col, lambda kept, d=d: t_shard(d, kept).start())
     for s in range(sections):
         pl.when(lower[s])(lambda s=s: factor_copy(s).start())
 
@@ -118,13 +141,21 @@
             product = dot3(halves(vectors), halves(tree_t[s]), ((1,), (1,)))
             node_v[s, 0], node_v[s, 1] = halves(product)
 
-    for which in range(2):
-        for d in range(1, peers):
-            gather_copy(which, d).wait_recv()
-    all_y_t = gather_y[...]
-    y_t[0], y_t[1] = halves(all_y_t)
-    product = dot3(halves(all_y_t.T), halves(gather_t[...]))
-    v[0], v[1] = halves(product)
+    for d in range(peers):
+        owner = lax.rem(col - d + peers, peers)
+        if d:
+            y_shard(d).wait_recv()
+        vectors = gather_y[of(owner), :]
+        y_t[0, of(owner), :], y_t[1, of(owner), :] = halves(vectors)
+        turned = halves(vectors.T)
+        if d:
+            by_shard(owner, lambda kept, d=d: t_shard(d, kept).wait_recv())
+        term = dot3(turned, halves(gather_t[of(owner), :]))
+        total = v_sum[...] + term if d else term
+        if d < peers - 1:
+            v_sum[...] = total
+        else:
+            v[0], v[1] = halves(total)
 
     def send_part(s, c, rows):
         part_out[s, c] = dot3((node_y_t[s, 0], node_y_t[s, 1]), halves(rows))
@@ -152,7 +183,7 @@
         else:
             head_copy(c).start()
 
-    lag = [1 + 2 * s for s in range(sections)]
+    lag = [1 + (s and 1 + 2 * s) for s in range(sections)]
 
     def step(t, carry):
         pl.when(t < chunks)(lambda: leaf(t))
@@ -172,11 +203,27 @@
         return carry
 
     lax.fori_loop(0, chunks, finish, 0)
-    for which in range(2):
-        for d in range(1, peers):
-            gather_copy(which, d).wait_send()
+    for d in range(1, peers):
+        y_shard(d).wait_send()
+        by_shard(col, lambda kept, d=d: t_shard(d, kept).wait_send())
     for s in range(sections):
         pl.when(lower[s])(lambda s=s: factor_copy(s).wait_send())
+
+
+def place(bands, band, mixed_hbm, out_hbm, held, in_sem, out_sem):
+    def copy_in(b):
+        return pltpu.make_async_copy(mixed_hbm.at[pl.ds(b * band, band)], held.at[b], in_sem.at[b])
+
+    def copy_out(b):
+        return pltpu.make_async_copy(held.at[b], out_hbm.at[pl.ds(b * band, band)], out_sem.at[b])
+
+    for b in range(bands):
+        copy_in(b).start()
+    for b in range(bands):
+        copy_in(b).wait()
+        copy_out(b).start()
+    for b in range(bands):
+        copy_out(b).wait()
 
 
 def shards(slab, leaf_y, leaf_t, tree_y, tree_t):
@@ -188,15 +235,15 @@
     chunks = cols // chunk_cols
     f32, bf16 = jnp.float32, jnp.bfloat16
     sizes = (peers, sections, chunks, width, chunk_cols, shard)
-    any_space = pl.BlockSpec(memory_space=pl.ANY)
     vmem = pl.BlockSpec(memory_space=pltpu.VMEM)
     dma = pltpu.SemaphoreType.DMA
     flops = 4 * cols * width * (rows + sections * width) * 3
-    return pl.pallas_call(
+    hbm = pl.BlockSpec(memory_space=pltpu.HBM)
+    mixed = pl.pallas_call(
         functools.partial(kernel, sizes),
         out_shape=jax.ShapeDtypeStruct(slab.shape, f32),
-        in_specs=[any_space, vmem, vmem, any_space, any_space],
-        out_specs=any_space,
+        in_specs=[hbm, vmem, vmem, hbm, hbm],
+        out_specs=hbm,
         scratch_shapes=[
             pltpu.VMEM((chunks, rows, chunk_cols), f32),
             pltpu.VMEM((chunks, width, chunk_cols), f32),
@@ -208,6 +255,7 @@
             pltpu.VMEM((width, width), f32),
             pltpu.VMEM((2, width, rows), bf16),
             pltpu.VMEM((2, rows, width), bf16),
+            pltpu.VMEM((rows, width), f32),
             pltpu.VMEM((sections, 2, width, width), bf16),
             pltpu.VMEM((sections, 2, width, width), bf16),
             dma((chunks,)),
@@ -222,12 +270,21 @@
             dma((2, peers)),
         ],
         compiler_params=pltpu.CompilerParams(
-            collective_id=0, has_side_effects=True, vmem_limit_bytes=52 * 2**20
+            collective_id=0, has_side_effects=True, vmem_limit_bytes=57 * 2**20
         ),
         cost_estimate=pl.CostEstimate(
             flops=flops, bytes_accessed=8 * rows * cols, transcendentals=0
         ),
-    )(slab, leaf_y, leaf_t, tree_y, tree_t)
+    )(slab, leaf_y.T, leaf_t.T, tree_y, tree_t)
+    bands = next(count for count in (16, 8, 4, 2, 1) if rows % (8 * count) == 0)
+    return pl.pallas_call(
+        functools.partial(place, bands, rows // bands),
+        out_shape=jax.ShapeDtypeStruct(slab.shape, f32),
+        in_specs=[hbm],
+        out_specs=hbm,
+        scratch_shapes=[pltpu.VMEM((bands, rows // bands, cols), f32), dma((bands,)), dma((bands,))],
+        compiler_params=pltpu.CompilerParams(vmem_limit_bytes=57 * 2**20),
+    )(mixed)
 
 
 def solution(mesh):

time: 74.9 us -> 71.8 us (0.959)
  local copies, waits for them, and re-layouts: 9.41 us -> 0 us
  Pallas kernels: 65.1 us -> 71.6 us
    unnamed x7 -> x0, local copies, waits for them, and re-layouts: 9.41 us -> none
    pallas_call x0 -> x1, Pallas kernels: none -> 4.93 us  [shards(): pl.pallas_call(functools.partial(place, bands, rows // bands), out_shape=...]
    pallas_call x1, Pallas kernels: 65.1 us -> 66.7 us  [shards(): pl.pallas_call(functools.partial(kernel, sizes), out_shape=jax.ShapeDtype...]
where the time goes in v2:
time: 71.8 us; the launch traced here: 71.6 us
  Pallas kernels  71.6 us (100%)
    pallas_call x1, Pallas kernels, shards(): pl.pallas_call(functools.partial(kernel, sizes), out_shape=jax.ShapeDtype...  66.7 us
    pallas_call x1, Pallas kernels, shards(): pl.pallas_call(functools.partial(place, bands, rows // bands), out_shape=...  4.93 us

profile of v2, /device:TPU:0, one launch (start us, length us, event | category | flops | bytes accessed | tf_op | source)
XLA Modules:
  0.0 71.6 jit_solution(10642396562525122963)
XLA Ops:
  0.0 66.7 %shard_map.55.mixed_hbm = f32[512,2560]{1,0:T(8,128)} custom-call(f32[512,2560]{1,0:T(8,128)} %slab_hbm.1, f32[64,512]{1,0:T(8,128)} %bitcast.2, f32[64,256]{1,0:T(8,128)} %bitcast.3, f32[3,256,256]{2,1,0:T(8,128)} %tree_y_hbm.1, f32[3,256,256]{2,1,0:T(8,128)} %tree_t_hbm.1), custom_call_target="tpu_custom_call" | custom-call | flops 10066329600 | bytes 10485760 | tf_op jit(solution)/shard_map/pallas_call | solution.py:242
  66.7 4.9 %shard_map.56 = f32[512,2560]{1,0:T(8,128)} custom-call(f32[512,2560]{1,0:T(8,128)} %shard_map.55.mixed_hbm), custom_call_target="tpu_custom_call" | custom-call | tf_op jit(solution)/shard_map/pallas_call | solution.py:280

commit v3 on v2

--- a/solution.py
+++ b/solution.py
@@ -15,16 +15,23 @@
     return high, (x - high.astype(jnp.float32)).astype(jnp.bfloat16)
 
 
-def dot3(left, right, dims=((1,), (0,))):
-    def one(a, b):
-        return lax.dot_general(a, b, (dims, ((), ())), preferred_element_type=jnp.float32)
-
-    return one(left[0], right[0]) + (one(left[0], right[1]) + one(left[1], right[0]))
+def wide(x):
+    high, low = halves(x)
+    return jnp.concatenate([high, high, low], axis=1)
+
+
+def tall(x):
+    high, low = halves(x)
+    return jnp.concatenate([high, low, high], axis=0)
+
+
+def product(left, right, dims=((1,), (0,))):
+    return lax.dot_general(left, right, (dims, ((), ())), preferred_element_type=jnp.float32)
 
 
 def kernel(
     sizes,
-    slab_hbm, leaf_y, leaf_t, tree_y_hbm, tree_t_hbm,
+    slab_hbm, leaf_y_hbm, leaf_t_hbm, tree_y_hbm, tree_t_hbm,
     out_hbm,
     slab, head, part_out, part_in, tree_y, tree_t,
     gather_y, gather_t, y_t, v, v_sum, node_y_t, node_v,
@@ -106,18 +113,22 @@
     for s in range(sections):
         pl.semaphore_signal(barrier, inc=1, device_id={"row": partner[s]}, device_id_type=MESH)
 
-    y_copy = pltpu.make_async_copy(tree_y_hbm, tree_y, y_sem)
-    y_copy.start()
-    for s in range(sections):
-        pl.when(lower[s])(lambda s=s: factor_local(s).start())
-    for c in range(chunks):
-        slab_copy(c).start()
+    own = [
+        pltpu.make_async_copy(leaf_y_hbm, gather_y.at[of(col)], y_sem.at[1]),
+        pltpu.make_async_copy(leaf_t_hbm, gather_t.at[of(col)], y_sem.at[2]),
+    ]
+    y_copy = pltpu.make_async_copy(tree_y_hbm, tree_y, y_sem.at[0])
     if short:
         gather_t[pl.ds(0, width // 2), pl.ds(width // 2, width // 2)] = jnp.zeros(
             (width // 2, width // 2), jnp.float32
         )
-    gather_y[of(col), :] = leaf_y[...]
-    gather_t[of(col), :] = leaf_t[...]
+    for copy in own:
+        copy.start()
+    y_copy.start()
+    for s in range(sections):
+        pl.when(lower[s])(lambda s=s: factor_local(s).start())
+    for copy in own:
+        copy.wait()
 
     pl.semaphore_wait(barrier, peers - 1 + sections)
     for d in range(1, peers):
@@ -127,6 +138,9 @@
     for s in range(sections):
         pl.when(lower[s])(lambda s=s: factor_copy(s).start())
 
+    for c in range(chunks):
+        slab_copy(c).start()
+
     y_copy.wait()
     for s in range(sections):
         pl.when(lower[s])(lambda s=s: factor_local(s).wait())
@@ -137,35 +151,36 @@
         @pl.when(active[s])
         def _(s=s):
             vectors = tree_y[s]
-            node_y_t[s, 0], node_y_t[s, 1] = halves(vectors.T)
-            product = dot3(halves(vectors), halves(tree_t[s]), ((1,), (1,)))
-            node_v[s, 0], node_v[s, 1] = halves(product)
+            node_y_t[s] = wide(vectors.T)
+            high, low = halves(tree_t[s])
+            factor = jnp.concatenate([high, low, high], axis=1)
+            node_v[s] = wide(product(wide(vectors), factor, ((1,), (1,))))
 
     for d in range(peers):
         owner = lax.rem(col - d + peers, peers)
         if d:
             y_shard(d).wait_recv()
         vectors = gather_y[of(owner), :]
-        y_t[0, of(owner), :], y_t[1, of(owner), :] = halves(vectors)
-        turned = halves(vectors.T)
+        y_t[of(owner), :] = wide(vectors)
+        turned = wide(vectors.T)
         if d:
             by_shard(owner, lambda kept, d=d: t_shard(d, kept).wait_recv())
-        term = dot3(turned, halves(gather_t[of(owner), :]))
+        term = product(turned, tall(gather_t[of(owner), :]))
         total = v_sum[...] + term if d else term
         if d < peers - 1:
             v_sum[...] = total
         else:
-            v[0], v[1] = halves(total)
+            v[...] = wide(total)
 
     def send_part(s, c, rows):
-        part_out[s, c] = dot3((node_y_t[s, 0], node_y_t[s, 1]), halves(rows))
+        part_out[s, c] = product(node_y_t[s], tall(rows))
         part_copy(s, c).start()
 
     def leaf(c):
         slab_copy(c).wait()
         block = slab[c]
-        coeffs = dot3((y_t[0], y_t[1]), halves(block))
-        updated = block - dot3((v[0], v[1]), halves(coeffs))
+        coeffs = product(y_t[...], tall(block))
+        updated = block - product(v[...], tall(coeffs))
         rows = updated[:width]
         head[c] = rows
         slab[c, width:, :] = updated[width:]
@@ -175,7 +190,7 @@
     def node(s, c):
         part_copy(s, c).wait_recv()
         coeffs = part_out[s, c] + part_in[s, c]
-        rows = head[c] - dot3((node_v[s, 0], node_v[s, 1]), halves(coeffs))
+        rows = head[c] - product(node_v[s], tall(coeffs))
         head[c] = rows
         if s + 1 < sections:
             pl.when(active[s + 1])(lambda: send_part(s + 1, c, rows))
@@ -183,7 +198,7 @@
         else:
             head_copy(c).start()
 
-    lag = [1 + (s and 1 + 2 * s) for s in range(sections)]
+    lag = [1] + [3 + s for s in range(1, sections)]
 
     def step(t, carry):
         pl.when(t < chunks)(lambda: leaf(t))
@@ -235,14 +250,13 @@
     chunks = cols // chunk_cols
     f32, bf16 = jnp.float32, jnp.bfloat16
     sizes = (peers, sections, chunks, width, chunk_cols, shard)
-    vmem = pl.BlockSpec(memory_space=pltpu.VMEM)
     dma = pltpu.SemaphoreType.DMA
     flops = 4 * cols * width * (rows + sections * width) * 3
     hbm = pl.BlockSpec(memory_space=pltpu.HBM)
     mixed = pl.pallas_call(
         functools.partial(kernel, sizes),
         out_shape=jax.ShapeDtypeStruct(slab.shape, f32),
-        in_specs=[hbm, vmem, vmem, hbm, hbm],
+        in_specs=[hbm] * 5,
         out_specs=hbm,
         scratch_shapes=[
             pltpu.VMEM((chunks, rows, chunk_cols), f32),
@@ -253,16 +267,16 @@
             pltpu.VMEM(tree_t.shape, f32),
             pltpu.VMEM((width, rows), f32),
             pltpu.VMEM((width, width), f32),
-            pltpu.VMEM((2, width, rows), bf16),
-            pltpu.VMEM((2, rows, width), bf16),
+            pltpu.VMEM((width, 3 * rows), bf16),
+            pltpu.VMEM((rows, 3 * width), bf16),
             pltpu.VMEM((rows, width), f32),
-            pltpu.VMEM((sections, 2, width, width), bf16),
-            pltpu.VMEM((sections, 2, width, width), bf16),
+            pltpu.VMEM((sections, width, 3 * width), bf16),
+            pltpu.VMEM((sections, width, 3 * width), bf16),
             dma((chunks,)),
             dma((2, chunks)),
             dma((sections, chunks)),
             dma((sections, chunks)),
-            dma,
+            dma((3,)),
             dma((sections,)),
             dma((sections,)),
             dma((sections,)),

time: 71.8 us -> 77 us (1.072)
  Pallas kernels: 71.6 us -> 76.9 us
    pallas_call x1, Pallas kernels: 66.7 us -> 71.9 us  [shards(): pl.pallas_call(functools.partial(kernel, sizes), out_shape=jax.ShapeDtype...]
where the time goes in v3:
time: 77 us; the launch traced here: 76.9 us
  Pallas kernels  76.9 us (100%)
    pallas_call x1, Pallas kernels, shards(): pl.pallas_call(functools.partial(kernel, sizes), out_shape=jax.ShapeDtype...  71.9 us
    pallas_call x1, Pallas kernels, shards(): pl.pallas_call(functools.partial(place, bands, rows // bands), out_shape=...  4.93 us

profile of v3, /device:TPU:0, one launch (start us, length us, event | category | flops | bytes accessed | tf_op | source)
XLA Modules:
  0.0 76.9 jit_solution(3224303293774706080)
XLA Ops:
  0.0 71.9 %shard_map.55.mixed_hbm = f32[512,2560]{1,0:T(8,128)} custom-call(f32[512,2560]{1,0:T(8,128)} %slab_hbm.1, f32[64,512]{1,0:T(8,128)} %bitcast.2, f32[64,256]{1,0:T(8,128)} %bitcast.3, f32[3,256,256]{2,1,0:T(8,128)} %tree_y_hbm.1, f32[3,256,256]{2,1,0:T(8,128)} %tree_t_hbm.1), custom_call_target="tpu_custom_call" | custom-call | flops 10066329600 | bytes 10485760 | tf_op jit(solution)/shard_map/pallas_call | solution.py:256
  71.9 4.9 %shard_map.56 = f32[512,2560]{1,0:T(8,128)} custom-call(f32[512,2560]{1,0:T(8,128)} %shard_map.55.mixed_hbm), custom_call_target="tpu_custom_call" | custom-call | tf_op jit(solution)/shard_map/pallas_call | solution.py:294

commit v4 on v3

--- a/solution.py
+++ b/solution.py
@@ -148,10 +148,11 @@
             lambda s=s: factor_copy(s).wait_recv()
         )
 
+        node_y_t[s] = wide(tree_y[s].T)
+
         @pl.when(active[s])
         def _(s=s):
             vectors = tree_y[s]
-            node_y_t[s] = wide(vectors.T)
             high, low = halves(tree_t[s])
             factor = jnp.concatenate([high, low, high], axis=1)
             node_v[s] = wide(product(wide(vectors), factor, ((1,), (1,))))
@@ -172,43 +173,57 @@
         else:
             v[...] = wide(total)
 
-    def send_part(s, c, rows):
-        part_out[s, c] = product(node_y_t[s], tall(rows))
-        part_copy(s, c).start()
-
-    def leaf(c):
-        slab_copy(c).wait()
-        block = slab[c]
-        coeffs = product(y_t[...], tall(block))
-        updated = block - product(v[...], tall(coeffs))
-        rows = updated[:width]
-        head[c] = rows
-        slab[c, width:, :] = updated[width:]
-        tail_copy(c).start()
-        send_part(0, c, rows)
-
-    def node(s, c):
-        part_copy(s, c).wait_recv()
-        coeffs = part_out[s, c] + part_in[s, c]
-        rows = head[c] - product(node_v[s], tall(coeffs))
-        head[c] = rows
-        if s + 1 < sections:
-            pl.when(active[s + 1])(lambda: send_part(s + 1, c, rows))
-            pl.when(jnp.logical_not(active[s + 1]))(lambda: head_copy(c).start())
-        else:
-            head_copy(c).start()
-
-    lag = [1] + [3 + s for s in range(1, sections)]
+    def work(leaf_chunk, nodes):
+        if leaf_chunk is not None:
+            slab_copy(leaf_chunk).wait()
+        for s, c in nodes:
+            part_copy(s, c).wait_recv()
+        held = [(part_out[s, c] + part_in[s, c], head[c]) for s, c in nodes]
+        block = None if leaf_chunk is None else slab[leaf_chunk]
+
+        done = []
+        for (s, c), (coeffs, rows) in zip(nodes, held):
+            rows = rows - product(node_v[s], tall(coeffs))
+            part = product(node_y_t[s + 1], tall(rows)) if s + 1 < sections else None
+            done.append((rows, part))
+        if leaf_chunk is not None:
+            coeffs = product(y_t[...], tall(block))
+            updated = block - product(v[...], tall(coeffs))
+            leaf_part = product(node_y_t[0], tall(updated[:width]))
+
+        for (s, c), (rows, part) in zip(nodes, done):
+            head[c] = rows
+            if part is None:
+                head_copy(c).start()
+                continue
+            part_out[s + 1, c] = part
+            pl.when(active[s + 1])(lambda s=s, c=c: part_copy(s + 1, c).start())
+            pl.when(jnp.logical_not(active[s + 1]))(lambda c=c: head_copy(c).start())
+        if leaf_chunk is not None:
+            head[leaf_chunk] = updated[:width]
+            part_out[0, leaf_chunk] = leaf_part
+            part_copy(0, leaf_chunk).start()
+            slab[leaf_chunk, width:, :] = updated[width:]
+            tail_copy(leaf_chunk).start()
+
+    lag = [3 * s for s in range(sections)]
+    both = jnp.logical_and
+    work(0, [])
 
     def step(t, carry):
-        pl.when(t < chunks)(lambda: leaf(t))
-        for s in range(sections):
-            c = t - lag[s]
-            inside = jnp.logical_and(c >= 0, c < chunks)
-            pl.when(jnp.logical_and(active[s], inside))(lambda s=s, c=c: node(s, c))
+        pl.when(t < chunks)(lambda: work(t, [(0, t - 1)]))
+        pl.when(t == chunks)(lambda: work(None, [(0, t - 1)]))
+        nodes = [(s, t - lag[s]) for s in range(1, sections)]
+        inside = [both(c >= 0, c < chunks) for _, c in nodes]
+        if nodes:
+            every = functools.reduce(both, inside, active[sections - 1])
+            pl.when(every)(lambda: work(None, nodes))
+            for (s, c), within in zip(nodes, inside):
+                alone = both(both(active[s], within), jnp.logical_not(every))
+                pl.when(alone)(lambda s=s, c=c: work(None, [(s, c)]))
         return carry
 
-    lax.fori_loop(0, chunks + lag[-1], step, 0)
+    lax.fori_loop(1, chunks + max(lag[-1], 1), step, 0)
 
     def finish(c, carry):
         tail_copy(c).wait()

time: 77 us -> 71.4 us (0.927)
  Pallas kernels: 76.9 us -> 71.3 us
    pallas_call x1, Pallas kernels: 71.9 us -> 66.3 us  [shards(): pl.pallas_call(functools.partial(kernel, sizes), out_shape=jax.ShapeDtype...]
where the time goes in v4:
time: 71.4 us; the launch traced here: 71.3 us
  Pallas kernels  71.3 us (100%)
    pallas_call x1, Pallas kernels, shards(): pl.pallas_call(functools.partial(kernel, sizes), out_shape=jax.ShapeDtype...  66.3 us
    pallas_call x1, Pallas kernels, shards(): pl.pallas_call(functools.partial(place, bands, rows // bands), out_shape=...  4.93 us

profile of v4, /device:TPU:0, one launch (start us, length us, event | category | flops | bytes accessed | tf_op | source)
XLA Modules:
  0.0 71.3 jit_solution(17602559566203683075)
XLA Ops:
  0.0 66.3 %shard_map.55.mixed_hbm = f32[512,2560]{1,0:T(8,128)} custom-call(f32[512,2560]{1,0:T(8,128)} %slab_hbm.1, f32[64,512]{1,0:T(8,128)} %bitcast.2, f32[64,256]{1,0:T(8,128)} %bitcast.3, f32[3,256,256]{2,1,0:T(8,128)} %tree_y_hbm.1, f32[3,256,256]{2,1,0:T(8,128)} %tree_t_hbm.1), custom_call_target="tpu_custom_call" | custom-call | flops 10066329600 | bytes 10485760 | tf_op jit(solution)/shard_map/pallas_call | solution.py:271
  66.3 4.9 %shard_map.56 = f32[512,2560]{1,0:T(8,128)} custom-call(f32[512,2560]{1,0:T(8,128)} %shard_map.55.mixed_hbm), custom_call_target="tpu_custom_call" | custom-call | tf_op jit(solution)/shard_map/pallas_call | solution.py:309

commit v5 on v4

--- a/solution.py
+++ b/solution.py
@@ -82,20 +82,17 @@
     def of(owner):
         return pl.ds(pl.multiple_of(owner * shard, shard), shard)
 
-    def y_shard(d):
-        return pltpu.make_async_remote_copy(
-            src_ref=gather_y.at[of(col)], dst_ref=gather_y.at[of(col)],
-            send_sem=gather_send.at[0, d], recv_sem=gather_recv.at[0, d],
-            device_id={"col": lax.rem(col + d, peers)}, device_id_type=MESH,
-        )
-
-    def t_shard(d, kept):
-        block = gather_t.at[of(col), pl.ds(0, kept)]
+    def shard_copy(which, owner, way, to, kept=None):
+        block = gather_t.at[of(owner), pl.ds(0, kept)] if which else gather_y.at[of(owner)]
         return pltpu.make_async_remote_copy(
             src_ref=block, dst_ref=block,
-            send_sem=gather_send.at[1, d], recv_sem=gather_recv.at[1, d],
-            device_id={"col": lax.rem(col + d, peers)}, device_id_type=MESH,
-        )
+            send_sem=gather_send.at[which, way, owner], recv_sem=gather_recv.at[which, owner],
+            device_id={"col": to}, device_id_type=MESH,
+        )
+
+    ahead = [col + 1, col - 1]
+    behind = [col - 1, col + 1]
+    open_way = [col < peers - 1, col > 0]
 
     def by_shard(owner, act):
         if short:
@@ -104,6 +101,24 @@
             pl.when(jnp.logical_not(early))(lambda: act(width))
         else:
             act(width)
+
+    def shard_send(which, owner, way):
+        def start(kept=None):
+            shard_copy(which, owner, way, ahead[way], kept).start()
+
+        pl.when(open_way[way])(lambda: by_shard(owner, start) if which else start())
+
+    def shard_sent(which, owner, way):
+        def wait(kept=None):
+            shard_copy(which, owner, way, ahead[way], kept).wait_send()
+
+        pl.when(open_way[way])(lambda: by_shard(owner, wait) if which else wait())
+
+    def shard_arrived(which, owner, way):
+        def wait(kept=None):
+            shard_copy(which, owner, way, behind[way], kept).wait_recv()
+
+        by_shard(owner, wait) if which else wait()
 
     barrier = pltpu.get_barrier_semaphore()
     for d in range(1, peers):
@@ -131,10 +146,9 @@
         copy.wait()
 
     pl.semaphore_wait(barrier, peers - 1 + sections)
-    for d in range(1, peers):
-        y_shard(d).start()
-    for d in range(1, peers):
-        by_shard(col, lambda kept, d=d: t_shard(d, kept).start())
+    for which in range(2):
+        for way in range(2):
+            shard_send(which, col, way)
     for s in range(sections):
         pl.when(lower[s])(lambda s=s: factor_copy(s).start())
 
@@ -157,21 +171,30 @@
             factor = jnp.concatenate([high, low, high], axis=1)
             node_v[s] = wide(product(wide(vectors), factor, ((1,), (1,))))
 
-    for d in range(peers):
-        owner = lax.rem(col - d + peers, peers)
-        if d:
-            y_shard(d).wait_recv()
+    def absorb(owner):
         vectors = gather_y[of(owner), :]
         y_t[of(owner), :] = wide(vectors)
-        turned = wide(vectors.T)
-        if d:
-            by_shard(owner, lambda kept, d=d: t_shard(d, kept).wait_recv())
-        term = product(turned, tall(gather_t[of(owner), :]))
-        total = v_sum[...] + term if d else term
-        if d < peers - 1:
-            v_sum[...] = total
-        else:
-            v[...] = wide(total)
+        return product(wide(vectors.T), tall(gather_t[of(owner), :]))
+
+    v_sum[...] = absorb(col)
+    for far in range(1, peers):
+        owners = [col - far, col + far]
+        there = [owners[0] >= 0, owners[1] < peers]
+        for which in range(2):
+            for way in range(2):
+
+                @pl.when(there[way])
+                def _(which=which, way=way, owner=owners[way]):
+                    shard_arrived(which, owner, way)
+                    shard_send(which, owner, way)
+
+        for way in range(2):
+
+            @pl.when(there[way])
+            def _(owner=owners[way]):
+                v_sum[...] += absorb(owner)
+
+    v[...] = wide(v_sum[...])
 
     def work(leaf_chunk, nodes):
         if leaf_chunk is not None:
@@ -233,27 +256,28 @@
         return carry
 
     lax.fori_loop(0, chunks, finish, 0)
-    for d in range(1, peers):
-        y_shard(d).wait_send()
-        by_shard(col, lambda kept, d=d: t_shard(d, kept).wait_send())
+    for which in range(2):
+        for way in range(2):
+            shard_sent(which, col, way)
+            for far in range(1, peers):
+                owner = (col - far, col + far)[way]
+                there = (owner >= 0, owner < peers)[way]
+                pl.when(there)(lambda a=(which, owner, way): shard_sent(*a))
     for s in range(sections):
         pl.when(lower[s])(lambda s=s: factor_copy(s).wait_send())
 
 
-def place(bands, band, mixed_hbm, out_hbm, held, in_sem, out_sem):
-    def copy_in(b):
-        return pltpu.make_async_copy(mixed_hbm.at[pl.ds(b * band, band)], held.at[b], in_sem.at[b])
-
-    def copy_out(b):
-        return pltpu.make_async_copy(held.at[b], out_hbm.at[pl.ds(b * band, band)], out_sem.at[b])
-
-    for b in range(bands):
-        copy_in(b).start()
-    for b in range(bands):
-        copy_in(b).wait()
-        copy_out(b).start()
-    for b in range(bands):
-        copy_out(b).wait()
+def place(bands, band, mixed_hbm, out_hbm, sem):
+    copies = [
+        pltpu.make_async_copy(
+            mixed_hbm.at[pl.ds(b * band, band)], out_hbm.at[pl.ds(b * band, band)], sem.at[b]
+        )
+        for b in range(bands)
+    ]
+    for copy in copies:
+        copy.start()
+    for copy in copies:
+        copy.wait()
 
 
 def shards(slab, leaf_y, leaf_t, tree_y, tree_t):
@@ -295,7 +319,7 @@
             dma((sections,)),
             dma((sections,)),
             dma((sections,)),
-            dma((2, peers)),
+            dma((2, 2, peers)),
             dma((2, peers)),
         ],
         compiler_params=pltpu.CompilerParams(
@@ -311,7 +335,7 @@
         out_shape=jax.ShapeDtypeStruct(slab.shape, f32),
         in_specs=[hbm],
         out_specs=hbm,
-        scratch_shapes=[pltpu.VMEM((bands, rows // bands, cols), f32), dma((bands,)), dma((bands,))],
+        scratch_shapes=[dma((bands,))],
         compiler_params=pltpu.CompilerParams(vmem_limit_bytes=57 * 2**20),
     )(mixed)
 

time: 71.4 us -> 223 us (3.12)
  Pallas kernels: 71.3 us -> 223 us
    pallas_call x1, Pallas kernels: 4.93 us -> 160 us  [shards(): pl.pallas_call(functools.partial(place, bands, rows // bands), out_shape=...]
    pallas_call x1, Pallas kernels: 66.3 us -> 63.1 us  [shards(): pl.pallas_call(functools.partial(kernel, sizes), out_shape=jax.ShapeDtype...]
where the time goes in v5:
time: 223 us
  Pallas kernels  223 us (100%)
    pallas_call x1, Pallas kernels, shards(): pl.pallas_call(functools.partial(place, bands, rows // bands), out_shape=...  160 us
    pallas_call x1, Pallas kernels, shards(): pl.pallas_call(functools.partial(kernel, sizes), out_shape=jax.ShapeDtype...  63.1 us

profile of v5, /device:TPU:0, one launch (start us, length us, event | category | flops | bytes accessed | tf_op | source)
XLA Modules:
  0.0 223.2 jit_solution(1587776812710401862)
XLA Ops:
  0.0 63.1 %shard_map.55.mixed_hbm = f32[512,2560]{1,0:T(8,128)} custom-call(f32[512,2560]{1,0:T(8,128)} %slab_hbm.1, f32[64,512]{1,0:T(8,128)} %bitcast.2, f32[64,256]{1,0:T(8,128)} %bitcast.3, f32[3,256,256]{2,1,0:T(8,128)} %tree_y_hbm.1, f32[3,256,256]{2,1,0:T(8,128)} %tree_t_hbm.1), custom_call_target="tpu_custom_call" | custom-call | flops 10066329600 | bytes 10485760 | tf_op jit(solution)/shard_map/pallas_call | solution.py:295
  63.1 160.1 %shard_map.56 = f32[512,2560]{1,0:T(8,128)} custom-call(f32[512,2560]{1,0:T(8,128)} %shard_map.55.mixed_hbm), custom_call_target="tpu_custom_call" | custom-call | tf_op jit(solution)/shard_map/pallas_call | solution.py:333

commit v6 on v5

--- a/solution.py
+++ b/solution.py
@@ -33,7 +33,7 @@
     sizes,
     slab_hbm, leaf_y_hbm, leaf_t_hbm, tree_y_hbm, tree_t_hbm,
     out_hbm,
-    slab, head, part_out, part_in, tree_y, tree_t,
+    slab, slab_tall, head, part_out, part_in, tree_y, tree_t,
     gather_y, gather_t, y_t, v, v_sum, node_y_t, node_v,
     slab_sem, out_sem, part_send, part_recv, y_sem,
     t_local, t_send, t_recv, gather_send, gather_recv,
@@ -176,6 +176,16 @@
         y_t[of(owner), :] = wide(vectors)
         return product(wide(vectors.T), tall(gather_t[of(owner), :]))
 
+    def split(first, last):
+        def one(c, carry):
+            slab_copy(c).wait()
+            slab_tall[c] = tall(slab[c])
+            return carry
+
+        lax.fori_loop(first, last, one, 0)
+
+    rounds = max(peers - 2, 1)
+    split_upto = [min(chunks, -(-chunks * far // rounds)) for far in range(peers)]
     v_sum[...] = absorb(col)
     for far in range(1, peers):
         owners = [col - far, col + far]
@@ -188,6 +198,7 @@
                     shard_arrived(which, owner, way)
                     shard_send(which, owner, way)
 
+        split(split_upto[far - 1], split_upto[far])
         for way in range(2):
 
             @pl.when(there[way])
@@ -197,8 +208,6 @@
     v[...] = wide(v_sum[...])
 
     def work(leaf_chunk, nodes):
-        if leaf_chunk is not None:
-            slab_copy(leaf_chunk).wait()
         for s, c in nodes:
             part_copy(s, c).wait_recv()
         held = [(part_out[s, c] + part_in[s, c], head[c]) for s, c in nodes]
@@ -210,7 +219,7 @@
             part = product(node_y_t[s + 1], tall(rows)) if s + 1 < sections else None
             done.append((rows, part))
         if leaf_chunk is not None:
-            coeffs = product(y_t[...], tall(block))
+            coeffs = product(y_t[...], slab_tall[leaf_chunk])
             updated = block - product(v[...], tall(coeffs))
             leaf_part = product(node_y_t[0], tall(updated[:width]))
 
@@ -267,17 +276,23 @@
         pl.when(lower[s])(lambda s=s: factor_copy(s).wait_send())
 
 
-def place(bands, band, mixed_hbm, out_hbm, sem):
-    copies = [
-        pltpu.make_async_copy(
-            mixed_hbm.at[pl.ds(b * band, band)], out_hbm.at[pl.ds(b * band, band)], sem.at[b]
-        )
-        for b in range(bands)
-    ]
-    for copy in copies:
-        copy.start()
-    for copy in copies:
-        copy.wait()
+def place(bands, band, mixed_hbm, out_hbm, held, in_sem, out_sem):
+    def copy_in(b):
+        return pltpu.make_async_copy(mixed_hbm.at[pl.ds(b * band, band)], held.at[b], in_sem.at[b])
+
+    def copy_out(b):
+        return pltpu.make_async_copy(held.at[b], out_hbm.at[pl.ds(b * band, band)], out_sem.at[b])
+
+    window = min(8, bands)
+    for b in range(window):
+        copy_in(b).start()
+    for b in range(bands):
+        copy_in(b).wait()
+        copy_out(b).start()
+        if b + window < bands:
+            copy_in(b + window).start()
+    for b in range(bands):
+        copy_out(b).wait()
 
 
 def shards(slab, leaf_y, leaf_t, tree_y, tree_t):
@@ -299,6 +314,7 @@
         out_specs=hbm,
         scratch_shapes=[
             pltpu.VMEM((chunks, rows, chunk_cols), f32),
+            pltpu.VMEM((chunks, 3 * rows, chunk_cols), bf16),
             pltpu.VMEM((chunks, width, chunk_cols), f32),
             pltpu.VMEM((sections, chunks, width, chunk_cols), f32),
             pltpu.VMEM((sections, chunks, width, chunk_cols), f32),
@@ -335,7 +351,7 @@
         out_shape=jax.ShapeDtypeStruct(slab.shape, f32),
         in_specs=[hbm],
         out_specs=hbm,
-        scratch_shapes=[dma((bands,))],
+        scratch_shapes=[pltpu.VMEM((bands, rows // bands, cols), f32), dma((bands,)), dma((bands,))],
         compiler_params=pltpu.CompilerParams(vmem_limit_bytes=57 * 2**20),
     )(mixed)
 

time: 223 us -> 68.1 us (0.31)
  Pallas kernels: 223 us -> 67.9 us
    pallas_call x1, Pallas kernels: 160 us -> 4.87 us  [shards(): pl.pallas_call(functools.partial(place, bands, rows // bands), out_shape=...]
where the time goes in v6:
time: 68.1 us; the launch traced here: 67.9 us
  Pallas kernels  67.9 us (100%)
    pallas_call x1, Pallas kernels, shards(): pl.pallas_call(functools.partial(kernel, sizes), out_shape=jax.ShapeDtype...  63 us
    pallas_call x1, Pallas kernels, shards(): pl.pallas_call(functools.partial(place, bands, rows // bands), out_shape=...  4.87 us

profile of v6, /device:TPU:0, one launch (start us, length us, event | category | flops | bytes accessed | tf_op | source)
XLA Modules:
  0.0 67.9 jit_solution(12518169777512076910)
XLA Ops:
  0.0 63.0 %shard_map.55.mixed_hbm = f32[512,2560]{1,0:T(8,128)} custom-call(f32[512,2560]{1,0:T(8,128)} %slab_hbm.1, f32[64,512]{1,0:T(8,128)} %bitcast.2, f32[64,256]{1,0:T(8,128)} %bitcast.3, f32[3,256,256]{2,1,0:T(8,128)} %tree_y_hbm.1, f32[3,256,256]{2,1,0:T(8,128)} %tree_t_hbm.1), custom_call_target="tpu_custom_call" | custom-call | flops 10066329600 | bytes 10485760 | tf_op jit(solution)/shard_map/pallas_call | solution.py:310
  63.0 4.9 %shard_map.56 = f32[512,2560]{1,0:T(8,128)} custom-call(f32[512,2560]{1,0:T(8,128)} %shard_map.55.mixed_hbm), custom_call_target="tpu_custom_call" | custom-call | tf_op jit(solution)/shard_map/pallas_call | solution.py:349

commit v7 on v6

--- a/solution.py
+++ b/solution.py
@@ -238,13 +238,14 @@
             slab[leaf_chunk, width:, :] = updated[width:]
             tail_copy(leaf_chunk).start()
 
-    lag = [3 * s for s in range(sections)]
+    lag = [1] + [3 * s - 1 for s in range(1, sections)]
     both = jnp.logical_and
-    work(0, [])
+    for c in range(min(2, chunks)):
+        work(c, [])
 
     def step(t, carry):
-        pl.when(t < chunks)(lambda: work(t, [(0, t - 1)]))
-        pl.when(t == chunks)(lambda: work(None, [(0, t - 1)]))
+        pl.when(t <= chunks)(lambda: work(None, [(0, t - 1)]))
+        pl.when(t + 1 < chunks)(lambda: work(t + 1, []))
         nodes = [(s, t - lag[s]) for s in range(1, sections)]
         inside = [both(c >= 0, c < chunks) for _, c in nodes]
         if nodes:
@@ -255,7 +256,7 @@
                 pl.when(alone)(lambda s=s, c=c: work(None, [(s, c)]))
         return carry
 
-    lax.fori_loop(1, chunks + max(lag[-1], 1), step, 0)
+    lax.fori_loop(1, chunks + lag[-1], step, 0)
 
     def finish(c, carry):
         tail_copy(c).wait()

time: 68.1 us -> 72.2 us (1.060)
  Pallas kernels: 67.9 us -> 71.9 us
    pallas_call x1, Pallas kernels: 63 us -> 67.1 us  [shards(): pl.pallas_call(functools.partial(kernel, sizes), out_shape=jax.ShapeDtype...]
where the time goes in v7:
time: 72.2 us; the launch traced here: 71.9 us
  Pallas kernels  71.9 us (100%)
    pallas_call x1, Pallas kernels, shards(): pl.pallas_call(functools.partial(kernel, sizes), out_shape=jax.ShapeDtype...  67.1 us
    pallas_call x1, Pallas kernels, shards(): pl.pallas_call(functools.partial(place, bands, rows // bands), out_shape=...  4.87 us

profile of v7, /device:TPU:0, one launch (start us, length us, event | category | flops | bytes accessed | tf_op | source)
XLA Modules:
  0.0 71.9 jit_solution(2157186807895748546)
XLA Ops:
  0.0 67.1 %shard_map.55.mixed_hbm = f32[512,2560]{1,0:T(8,128)} custom-call(f32[512,2560]{1,0:T(8,128)} %slab_hbm.1, f32[64,512]{1,0:T(8,128)} %bitcast.2, f32[64,256]{1,0:T(8,128)} %bitcast.3, f32[3,256,256]{2,1,0:T(8,128)} %tree_y_hbm.1, f32[3,256,256]{2,1,0:T(8,128)} %tree_t_hbm.1), custom_call_target="tpu_custom_call" | custom-call | flops 10066329600 | bytes 10485760 | tf_op jit(solution)/shard_map/pallas_call | solution.py:311
  67.1 4.9 %shard_map.56 = f32[512,2560]{1,0:T(8,128)} custom-call(f32[512,2560]{1,0:T(8,128)} %shard_map.55.mixed_hbm), custom_call_target="tpu_custom_call" | custom-call | tf_op jit(solution)/shard_map/pallas_call | solution.py:350

commit v8 on v6

--- a/solution.py
+++ b/solution.py
@@ -15,18 +15,17 @@
     return high, (x - high.astype(jnp.float32)).astype(jnp.bfloat16)
 
 
-def wide(x):
-    high, low = halves(x)
-    return jnp.concatenate([high, high, low], axis=1)
-
-
-def tall(x):
-    high, low = halves(x)
-    return jnp.concatenate([high, low, high], axis=0)
-
-
-def product(left, right, dims=((1,), (0,))):
-    return lax.dot_general(left, right, (dims, ((), ())), preferred_element_type=jnp.float32)
+def stacked(x):
+    return jnp.concatenate(halves(x), axis=0)
+
+
+def product(left, right):
+    def one(a, b):
+        return jnp.dot(a, b, preferred_element_type=jnp.float32)
+
+    rows, depth = left.shape[0] // 2, left.shape[1]
+    main = one(left, right[:depth])
+    return main[:rows] + (main[rows:] + one(left[:rows], right[depth:]))
 
 
 def kernel(
@@ -162,24 +161,22 @@
             lambda s=s: factor_copy(s).wait_recv()
         )
 
-        node_y_t[s] = wide(tree_y[s].T)
+        node_y_t[s] = stacked(tree_y[s].T)
 
         @pl.when(active[s])
         def _(s=s):
             vectors = tree_y[s]
-            high, low = halves(tree_t[s])
-            factor = jnp.concatenate([high, low, high], axis=1)
-            node_v[s] = wide(product(wide(vectors), factor, ((1,), (1,))))
+            node_v[s] = stacked(product(stacked(vectors), stacked(tree_t[s].T)))
 
     def absorb(owner):
         vectors = gather_y[of(owner), :]
-        y_t[of(owner), :] = wide(vectors)
-        return product(wide(vectors.T), tall(gather_t[of(owner), :]))
+        y_t[0, of(owner), :], y_t[1, of(owner), :] = halves(vectors)
+        return product(stacked(vectors.T), stacked(gather_t[of(owner), :]))
 
     def split(first, last):
         def one(c, carry):
             slab_copy(c).wait()
-            slab_tall[c] = tall(slab[c])
+            slab_tall[c] = stacked(slab[c])
             return carry
 
         lax.fori_loop(first, last, one, 0)
@@ -205,7 +202,7 @@
             def _(owner=owners[way]):
                 v_sum[...] += absorb(owner)
 
-    v[...] = wide(v_sum[...])
+    v[...] = stacked(v_sum[...])
 
     def work(leaf_chunk, nodes):
         for s, c in nodes:
@@ -215,13 +212,13 @@
 
         done = []
         for (s, c), (coeffs, rows) in zip(nodes, held):
-            rows = rows - product(node_v[s], tall(coeffs))
-            part = product(node_y_t[s + 1], tall(rows)) if s + 1 < sections else None
+            rows = rows - product(node_v[s], stacked(coeffs))
+            part = product(node_y_t[s + 1], stacked(rows)) if s + 1 < sections else None
             done.append((rows, part))
         if leaf_chunk is not None:
-            coeffs = product(y_t[...], slab_tall[leaf_chunk])
-            updated = block - product(v[...], tall(coeffs))
-            leaf_part = product(node_y_t[0], tall(updated[:width]))
+            coeffs = product(y_t[...].reshape(2 * width, -1), slab_tall[leaf_chunk])
+            updated = block - product(v[...], stacked(coeffs))
+            leaf_part = product(node_y_t[0], stacked(updated[:width]))
 
         for (s, c), (rows, part) in zip(nodes, done):
             head[c] = rows
@@ -314,7 +311,7 @@
         out_specs=hbm,
         scratch_shapes=[
             pltpu.VMEM((chunks, rows, chunk_cols), f32),
-            pltpu.VMEM((chunks, 3 * rows, chunk_cols), bf16),
+            pltpu.VMEM((chunks, 2 * rows, chunk_cols), bf16),
             pltpu.VMEM((chunks, width, chunk_cols), f32),
             pltpu.VMEM((sections, chunks, width, chunk_cols), f32),
             pltpu.VMEM((sections, chunks, width, chunk_cols), f32),
@@ -322,11 +319,11 @@
             pltpu.VMEM(tree_t.shape, f32),
             pltpu.VMEM((width, rows), f32),
             pltpu.VMEM((width, width), f32),
-            pltpu.VMEM((width, 3 * rows), bf16),
-            pltpu.VMEM((rows, 3 * width), bf16),
+            pltpu.VMEM((2, width, rows), bf16),
+            pltpu.VMEM((2 * rows, width), bf16),
             pltpu.VMEM((rows, width), f32),
-            pltpu.VMEM((sections, width, 3 * width), bf16),
-            pltpu.VMEM((sections, width, 3 * width), bf16),
+            pltpu.VMEM((sections, 2 * width, width), bf16),
+            pltpu.VMEM((sections, 2 * width, width), bf16),
             dma((chunks,)),
             dma((2, chunks)),
             dma((sections, chunks)),

time: 68.1 us -> 68.1 us (level)
  no operation moved by 1% of the time
where the time goes in v8:
time: 68.1 us; the launch traced here: 67.9 us
  Pallas kernels  67.9 us (100%)
    pallas_call x1, Pallas kernels, shards(): pl.pallas_call(functools.partial(kernel, sizes), out_shape=jax.ShapeDtype...  63 us
    pallas_call x1, Pallas kernels, shards(): pl.pallas_call(functools.partial(place, bands, rows // bands), out_shape=...  4.87 us

profile of v8, /device:TPU:0, one launch (start us, length us, event | category | flops | bytes accessed | tf_op | source)
XLA Modules:
  0.0 67.9 jit_solution(4155916821329675756)
XLA Ops:
  0.0 63.0 %shard_map.55.mixed_hbm = f32[512,2560]{1,0:T(8,128)} custom-call(f32[512,2560]{1,0:T(8,128)} %slab_hbm.1, f32[64,512]{1,0:T(8,128)} %bitcast.2, f32[64,256]{1,0:T(8,128)} %bitcast.3, f32[3,256,256]{2,1,0:T(8,128)} %tree_y_hbm.1, f32[3,256,256]{2,1,0:T(8,128)} %tree_t_hbm.1), custom_call_target="tpu_custom_call" | custom-call | flops 10066329600 | bytes 10485760 | tf_op jit(solution)/shard_map/pallas_call | solution.py:307
  63.0 4.9 %shard_map.56 = f32[512,2560]{1,0:T(8,128)} custom-call(f32[512,2560]{1,0:T(8,128)} %shard_map.55.mixed_hbm), custom_call_target="tpu_custom_call" | custom-call | tf_op jit(solution)/shard_map/pallas_call | solution.py:346
